TPU v7x, 512 devices: a whole 4x8x8 slice. The times are simulated.
512 devices in a mesh: row: 64 (over y, x, core), col: 8 (over z).
Axes of the slice: x: 4, y: 8, z: 8, core: 2. Of those that a mesh axis runs over, the one named last changes fastest.
Arguments:
- p_panel: bfloat16 [2, 512, 65536], P(None, 'col', 'row'), may hold values from -0.1875 to 0.1875
- h_panel: bfloat16 [2, 512, 8192], P(None, 'row', 'col'), may hold values from -6 to 6
- p_tile: bfloat16 [65536, 8192], P('row', 'col'), may hold values from -3 to 3
- p_mask: int32 [128, 2], replicated, may hold values 0 or 1
- h_mask: int32 [2, 16], replicated, may hold values 0 or 1
- keep_mask: int32 [128, 16], replicated, may hold values 0 or 1
Outputs:
- p_next: bfloat16 [65536, 8192], P('row', 'col')
All inputs are finite; a program needn't handle non-finite values.
Results may differ from a plain program's by a relative error of at most 0.001.
Values may be sent and summed in bfloat16 or wider, within the bound.
No kernel may reach another device: no remote copies, remote signals or barrier semaphores. Data moves between devices by JAX's collectives and lax.ppermute only.
A program may use at most 64 MiB of HBM per device.

v0:
```python
import jax
import jax.numpy as jnp
from jax import lax
from jax.sharding import PartitionSpec as P

B = 512
PANELS = 2


def contract(left_block, right_block):
    return lax.dot_general(
        left_block, right_block, (((0,), (0,)), ((), ())), preferred_element_type=jnp.float32
    )


def local(p_panel, h_panel, p_tile, p_mask, h_mask, keep_mask):
    row_count = p_panel.shape[2] // B
    col_count = h_panel.shape[2] // B
    row_first = lax.axis_index("row") * row_count
    col_first = lax.axis_index("col") * col_count
    row_alive = lax.dynamic_slice_in_dim(p_mask, row_first, row_count, 0)
    col_alive = lax.dynamic_slice_in_dim(h_mask, col_first, col_count, 1)
    keep_local = lax.dynamic_slice(keep_mask, (row_first, col_first), (row_count, col_count))
    p_scale = jnp.repeat(row_alive.T, B, axis=1).astype(jnp.bfloat16)
    h_scale = jnp.repeat(col_alive, B, axis=1).astype(jnp.bfloat16)
    p_masked = p_panel * p_scale[:, None, :]
    h_masked = h_panel * h_scale[:, None, :]

    def panel_term(panel_piece, h_rows):
        return contract(panel_piece, h_rows)

    running = jnp.zeros((p_panel.shape[2], h_panel.shape[2]), jnp.float32)
    for panel_id in range(PANELS):
        h_gathered = lax.all_gather(h_masked[panel_id], "row", axis=0, tiled=True)

        def add_piece(carried, panel_piece, offset, h_gathered=h_gathered, panel_id=panel_id):
            return carried + panel_term(panel_piece, h_gathered)

        running = add_piece(
            running, lax.all_gather(p_masked[panel_id], "col", axis=0, tiled=True), jnp.int32(0)
        )
    keep_full = jnp.repeat(jnp.repeat(keep_local, B, axis=0), B, axis=1).astype(jnp.float32)
    return (keep_full * (2.0 * p_tile.astype(jnp.float32) - running)).astype(jnp.bfloat16)


def solution(mesh):
    in_specs = (P(None, "col", "row"), P(None, "row", "col"), P("row", "col"), P(), P(), P())
    out_specs = P("row", "col")
    return jax.shard_map(local, mesh=mesh, in_specs=in_specs, out_specs=out_specs, check_vma=False)
```

profile of v0, /device:TPU:1, one launch (start us, length us, event | category | flops | bytes accessed | tf_op | source)
XLA Modules:
  0.0 279.2 jit_solution(17297307573320776223)
XLA Ops:
  6.5 0.0 all-gather.9.cloned.1.call-start
  6.5 0.8 dynamic-slice_convert_fusion.2
  7.3 0.1 broadcast_bitcast_fusion.1
  7.4 1.0 broadcast_multiply_fusion
  8.4 0.7 fusion.6
  9.1 0.0 all-gather.9.cloned.1.call-update
  9.1 0.0 all-gather.11.cloned.1.call-start
  9.2 0.8 dynamic-slice_convert_fusion
  9.9 0.1 broadcast_bitcast_fusion
  10.0 0.8 broadcast_multiply_fusion.1
  10.8 0.6 fusion.7
  11.4 0.0 all-gather.11.cloned.1.call-update
  11.4 0.0 all-gather.13.cloned.1.call-start
  11.4 0.7 all-gather.13.cloned.1.call-update
  12.1 0.0 all-gather.15.cloned.1.call-start
  12.2 0.5 all-gather.15.cloned.1.call-update
  12.7 0.1 copy.7
  12.8 1.4 broadcast_in_dim.15
  14.2 3.0 %copy.8 = f32[128,8,2,512]{3,1,2,0:T(8,128)} copy(f32[128,8,2,512]{3,2,1,0:T(2,128)S(1)} %bitcast.24) | data formatting | bytes 8388608
  17.2 0.0 copy-start
  17.2 35.4 %all-gather.9.cloned.1.call-done = bf16[1,512,1024]{2,1,0:T(8,128)(2,1)} async-done(((bf16[1,64,1024]{2,1,0:T(8,128)(2,1)}), bf16[1,512,1024]{2,1,0:T(8,128)(2,1)}) %all-gather.9.cloned.1.call-update) | async-done | bytes 1048592 | tf_op jit(solution)/shard_map/all_gather | solution.py:40
  52.6 88.0 %all-gather.11.cloned.1.call-done = bf16[1,512,1024]{2,1,0:T(8,128)(2,1)} async-done(((bf16[1,8,1024]{2,1,0:T(8,128)(2,1)}), bf16[1,512,1024]{2,1,0:T(8,128)(2,1)}) %all-gather.11.cloned.1.call-update) | async-done | bytes 1048592 | tf_op jit(solution)/shard_map/all_gather | solution.py:34
  140.6 4.8 %fusion.2 = f32[1024,1024]{1,0:T(8,128)} fusion(bf16[1,512,1024]{2,1,0:T(8,128)(2,1)} %all-gather.11.cloned.1.call-done, bf16[1,512,1024]{2,1,0:T(8,128)(2,1)} %all-gather.9.cloned.1.call-done), kind=kOutput, calls=%fused_computation.3 | convolution fusion | flops 1073741824 | bytes 6291456 | tf_op jit(solution)/shard_map/dot_general | solution.py:11
  145.3 32.6 %all-gather.13.cloned.1.call-done = bf16[1,512,1024]{2,1,0:T(8,128)(2,1)} async-done(((bf16[1,64,1024]{2,1,0:T(8,128)(2,1)}), bf16[1,512,1024]{2,1,0:T(8,128)(2,1)}) %all-gather.13.cloned.1.call-update) | async-done | bytes 1048592 | tf_op jit(solution)/shard_map/all_gather | solution.py:40
  177.9 87.8 %all-gather.15.cloned.1.call-done = bf16[1,512,1024]{2,1,0:T(8,128)(2,1)} async-done(((bf16[1,8,1024]{2,1,0:T(8,128)(2,1)}), bf16[1,512,1024]{2,1,0:T(8,128)(2,1)}) %all-gather.15.cloned.1.call-update) | async-done | bytes 1048592 | tf_op jit(solution)/shard_map/all_gather | solution.py:34
  265.8 0.0 copy-done
  265.8 6.9 %multiply_convert_fusion = bf16[1024,1024]{1,0:T(8,128)(2,1)} fusion(f32[1024,1024]{1,0:T(8,128)} %bitcast.23, f32[1024,1024]{1,0:T(8,128)} %fusion.2, bf16[1024,1024]{1,0:T(8,128)(2,1)S(1)} %copy-done, bf16[1,512,1024]{2,1,0:T(8,128)(2,1)} %all-gather.15.cloned.1.call-done, bf16[1,512,1024]{2,1,0:T(8,128)(2,1)} %all-gather.13.cloned.1.call-done), kind=kOutput, calls=%fused_computation | convolution fusion | flops 1080033280 | bytes 14680064 | tf_op jit(solution)/shard_map/dot_general | solution.py:11
  (3 shorter events, 0.1 us)
Async XLA Ops:
  6.5 46.0 %all-gather.9.cloned.1.call-start = ((), (), s32[]{:S(2)}) async-start(), calls=%async_computation | async-start | bytes 1179648 | tf_op jit(solution)/shard_map/all_gather | solution.py:40
  9.1 131.4 %all-gather.11.cloned.1.call-start = ((), (), s32[]{:S(2)}) async-start(), calls=%async_computation.1 | async-start | bytes 1064960 | tf_op jit(solution)/shard_map/all_gather | solution.py:34
  11.4 166.5 %all-gather.13.cloned.1.call-start = ((), (), s32[]{:S(2)}) async-start(), calls=%async_computation.2 | async-start | bytes 1179648 | tf_op jit(solution)/shard_map/all_gather | solution.py:40
  12.1 253.6 %all-gather.15.cloned.1.call-start = ((), (), s32[]{:S(2)}) async-start(), calls=%async_computation.3 | async-start | bytes 1064960 | tf_op jit(solution)/shard_map/all_gather | solution.py:34
  17.2 248.6 %copy-start = (bf16[1024,1024]{1,0:T(8,128)(2,1)S(1)}, bf16[1024,1024]{1,0:T(8,128)(2,1)}, u32[]{:S(2)}) copy-start(bf16[1024,1024]{1,0:T(8,128)(2,1)} %param.8) | copy-start | bytes 6291460
Sparse Core Ops, SparseCore 0:
  9.4 43.0 all-gather.8
  55.9 84.5 all-gather.10
  142.6 35.2 all-gather.12
  181.1 84.5 all-gather.14
where the time goes:
time: 279 us
  waiting for transfers between devices  245 us (88%)
  between operations  13.1 us (5%)
  matrix products  11.7 us (4%)
  local copies, waits for them, and re-layouts  5.97 us (2%)
  other arithmetic  3.27 us (1%)
    all_gather x2, waiting for transfers between devices, local(): h_gathered = lax.all_gather(h_masked[panel_id], 'row', axis=0, tiled=True)  176 us
    all_gather x2, waiting for transfers between devices, local(): lax.all_gather(p_masked[panel_id], 'col', axis=0, tiled=True)  68 us
    dot_general x2, matrix products, contract(): lax.dot_general(left_block, right_block, (((0,), (0,)), ((), ())), prefer...  11.7 us
  transfers between devices with their start and end apart: 4, of which 4 were waited for; matrix products, arithmetic and copies ran while one was open for 4% of the time, Pallas kernels for 0%

commit v1 on v0

v1 whole, which is shorter than its diff:
```python
import functools

import jax
import jax.numpy as jnp
from jax import lax
from jax.experimental import pallas as pl
from jax.experimental.pallas import tpu as pltpu
from jax.sharding import PartitionSpec as P

B = 512
PANELS = 2
CORES = 2


def finish(flags, p_ref, own_ref, other_ref, tile_ref, out_ref, *, rows):
    own = flags[0]
    other = 1 - own
    row_block = pl.program_id(0) * rows // B
    own_row = flags[1 + row_block * 2 + own]
    other_row = flags[1 + row_block * 2 + other]
    contract = (((0,), (0,)), ((), ()))
    for col in range(out_ref.shape[1] // B):
        cols = slice(col * B, (col + 1) * B)
        own_alive = (own_row * flags[5 + own * 2 + col]).astype(jnp.float32)
        other_alive = (other_row * flags[5 + other * 2 + col]).astype(jnp.float32)
        keep = flags[9 + row_block * 2 + col].astype(jnp.float32)
        product = own_alive * lax.dot_general(
            p_ref[own], own_ref[:, cols], contract, preferred_element_type=jnp.float32
        ) + other_alive * lax.dot_general(
            p_ref[other], other_ref[:, cols], contract, preferred_element_type=jnp.float32
        )
        tile = tile_ref[:, cols].astype(jnp.float32)
        out_ref[:, cols] = (keep * (2.0 * tile - product)).astype(out_ref.dtype)


def purify(flags, p_full, own, other, p_tile):
    rows = 256
    height, width = p_tile.shape
    inner = p_full.shape[1]
    return pl.pallas_call(
        functools.partial(finish, rows=rows),
        out_shape=jax.ShapeDtypeStruct((height, width), p_tile.dtype),
        grid=(height // rows,),
        in_specs=[
            pl.BlockSpec(memory_space=pltpu.SMEM),
            pl.BlockSpec((PANELS, inner, rows), lambda i: (0, 0, i)),
            pl.BlockSpec((inner, width), lambda i: (0, 0)),
            pl.BlockSpec((inner, width), lambda i: (0, 0)),
            pl.BlockSpec((rows, width), lambda i: (i, 0)),
        ],
        out_specs=pl.BlockSpec((rows, width), lambda i: (i, 0)),
        compiler_params=pltpu.CompilerParams(vmem_limit_bytes=40 << 20),
        cost_estimate=pl.CostEstimate(
            flops=2 * PANELS * inner * height * width,
            bytes_accessed=2 * (PANELS * inner * (height + width) + 2 * height * width),
            transcendentals=0,
        ),
    )(flags, p_full, own, other, p_tile)


def local(p_panel, h_panel, p_tile, p_mask, h_mask, keep_mask, *, row_devices):
    row_index = lax.axis_index("row")
    core = row_index % CORES
    p_full = lax.all_gather(p_panel, "col", axis=1, tiled=True)

    chips = row_devices // CORES
    pairs = [[CORES * chip + c for c in range(CORES)] for chip in range(chips)]
    planes = [[CORES * chip + c for chip in range(chips)] for c in range(CORES)]
    both = lax.all_gather(h_panel, "row", axis=1, axis_index_groups=pairs)
    mine = lax.dynamic_index_in_dim(both, core, 0, keepdims=False)
    mine = mine.reshape(-1, mine.shape[-1])
    spread = lax.all_to_all(
        jnp.broadcast_to(mine[None], (chips,) + mine.shape), "row", 0, 0, axis_index_groups=planes
    )
    own = spread.reshape(-1, mine.shape[-1])
    other = lax.ppermute(own, "row", [(d, d ^ 1) for d in range(row_devices)])

    row_count = p_tile.shape[0] // B
    col_count = p_tile.shape[1] // B
    row_first = row_index * row_count
    col_first = lax.axis_index("col") * col_count
    flags = jnp.concatenate(
        [
            core[None].astype(jnp.int32),
            lax.dynamic_slice_in_dim(p_mask, row_first, row_count, 0).reshape(-1),
            lax.dynamic_slice_in_dim(h_mask, col_first, col_count, 1).reshape(-1),
            lax.dynamic_slice(keep_mask, (row_first, col_first), (row_count, col_count)).reshape(-1),
        ]
    )
    return purify(flags, p_full, own, other, p_tile)


def solution(mesh):
    in_specs = (P(None, "col", "row"), P(None, "row", "col"), P("row", "col"), P(), P(), P())
    out_specs = P("row", "col")
    body = functools.partial(local, row_devices=mesh.shape["row"])
    return jax.shard_map(body, mesh=mesh, in_specs=in_specs, out_specs=out_specs, check_vma=False)
```

time: 279 us -> 73.1 us (0.26)
  the two profiles are of different devices: /device:TPU:1 before, /device:TPU:2 now
where the time goes in v1:
time: 73.1 us; the launch traced here: 72.9 us
  blocking collectives  40.7 us (56%)
  between operations  13.4 us (18%)
  waiting for transfers between devices  8.06 us (11%)
  Pallas kernels  5.6 us (8%)
  local copies, waits for them, and re-layouts  3.07 us (4%)
  starting transfers between devices  1.91 us (3%)
    all_to_all x1, blocking collectives, local(): lax.all_to_all(jnp.broadcast_to(mine[None], (chips,) + mine.shape), 'row'...  38.4 us
    all_gather x1, waiting for transfers between devices, local(): p_full = lax.all_gather(p_panel, 'col', axis=1, tiled=True)  6.04 us
    pallas_call x1, Pallas kernels, purify(): pl.pallas_call(functools.partial(finish, rows=rows), out_shape=jax.ShapeD...  5.6 us
    all_gather x1, blocking collectives, local(): both = lax.all_gather(h_panel, 'row', axis=1, axis_index_groups=pairs)  2.25 us
    ppermute x1, starting transfers between devices, local(): other = lax.ppermute(own, 'row', [(d, d ^ 1) for d in range(row_devices)])  1.91 us
    unnamed x8, local copies, waits for them, and re-layouts  1.6 us
  transfers between devices with their start and end apart: 2, of which 2 were waited for; matrix products, arithmetic and copies ran while one was open for 2% of the time, Pallas kernels for 0%

profile of v1, /device:TPU:2, one launch (start us, length us, event | category | flops | bytes accessed | tf_op | source)
XLA Modules:
  0.0 72.9 jit_solution(5116285602344186074)
XLA Ops:
  6.5 0.0 copy-start
  6.5 0.0 copy-start.3
  6.5 0.0 copy-start.1
  6.5 0.0 all-gather.3.cloned.1.call-start
  6.5 0.7 all-gather.3.cloned.1.call-update
  7.3 2.2 %all-gather = bf16[2,16,1024]{2,1,0:T(8,128)(2,1)S(1)} all-gather(bf16[2,8,1024]{2,1,0:T(8,128)(2,1)} %param.7), channel_id=2, replica_groups={{0,8},{16,24},{32,40},{48,56},{64,72},{80,88},{96,104},{112,120},{128,1..., dimensions={1}, use_global_device_ids=true | all-gather | bytes 98304 | tf_op jit(solution)/shard_map/all_gather | solution.py:69
  9.5 0.1 broadcast_in_dim.12
  9.7 38.4 %all_to_all.5 = bf16[32,16,1024]{2,1,0:T(8,128)(2,1)S(1)} all-to-all(bf16[32,16,1024]{2,1,0:T(8,128)(2,1)S(1)} %broadcast_in_dim.12), channel_id=1, replica_groups={{0,16,32,48,64,80,96,112,128,144,160,176,192,208,224,240,256,272,288,30..., dimensions={0} | all-to-all | bytes 2097152 | tf_op jit(solution)/shard_map/all_to_all | solution.py:72
  48.1 1.9 %collective-permute-start = (bf16[512,1024]{1,0:T(8,128)(2,1)S(1)}, bf16[512,1024]{1,0:T(8,128)(2,1)}, u32[]{:S(2)}, u32[]{:S(2)}) collective-permute-start(bf16[512,1024]{1,0:T(8,128)(2,1)S(1)} %bitcast.5), channel_id=1, source_target_pairs={{0,8},{8,0},{16,24},{24,16},{32,40},{40,32},{48,56},{56,48},{64,72... | collective-permute-start | bytes 3145736 | tf_op jit(solution)/shard_map/ppermute | solution.py:76
  50.0 0.0 copy-done
  50.0 0.1 constant_dynamic-slice_fusion.1
  50.1 0.1 copy.7
  50.2 0.1 reshape.14
  50.3 0.8 %dynamic_slice.15 = s32[2,2]{0,1:T(2,128)S(1)} dynamic-slice(s32[128,16]{0,1:T(8,128)} %param.11, s32[]{:T(128)S(6)} %select_n.20, s32[]{:T(128)S(6)} %select_n.21), dynamic_slice_sizes={2,2} | dynamic-slice | bytes 36 | tf_op jit(solution)/shard_map/dynamic_slice | solution.py:87
  51.1 0.1 copy.8
  51.1 0.1 reshape.16
  51.2 0.0 copy-done.3
  51.2 0.1 constant_dynamic-slice_fusion
  51.3 0.1 reshape.15
  51.4 0.1 pad_add_fusion.flags
  51.5 1.3 %collective-permute-done.other_ref = bf16[512,1024]{1,0:T(8,128)(2,1)} collective-permute-done((bf16[512,1024]{1,0:T(8,128)(2,1)S(1)}, bf16[512,1024]{1,0:T(8,128)(2,1)}, u32[]{:S(2)}, u32[]{:S(2)}) %collective-permute-start) | collective-permute-done | bytes 1048608 | tf_op jit(solution)/shard_map/ppermute | solution.py:76
  52.8 6.0 %all-gather.3.cloned.1.call-done.p_ref = bf16[2,512,1024]{2,1,0:T(8,128)(2,1)} async-done(((bf16[2,64,1024]{2,1,0:T(8,128)(2,1)}), bf16[2,512,1024]{2,1,0:T(8,128)(2,1)}) %all-gather.3.cloned.1.call-update) | async-done | bytes 2097168 | tf_op jit(solution)/shard_map/all_gather | solution.py:64
  58.8 0.0 copy-done.1
  58.8 0.0 copy-start.2
  58.8 1.6 %copy-done.2 = bf16[2,512,1024]{2,1,0:T(8,128)(2,1)S(1)} copy-done((bf16[2,512,1024]{2,1,0:T(8,128)(2,1)S(1)}, bf16[2,512,1024]{2,1,0:T(8,128)(2,1)}, u32[]{:S(2)}) %copy-start.2) | copy-done | bytes 2097176
  60.4 5.6 %shard_map.64 = bf16[1024,1024]{1,0:T(8,128)(2,1)} custom-call(s32[13]{0:T(128)S(1)} %pad_add_fusion.flags, bf16[2,512,1024]{2,1,0:T(8,128)(2,1)S(1)} %copy-done.2, bf16[512,1024]{1,0:T(8,128)(2,1)S(1)} %bitcast.6, bf16[512,1024]{1,0:T(8,128)(2,1)} %collective-permute-done.other_ref, bf16[1024,1024]{1,0:T(8,128)(2,1)S(1)} %copy-done.1), custom_call_target="tpu_custom_call" | custom-call | flops 2147483648 | bytes 8388608 | tf_op jit(solution)/shard_map/pallas_call | solution.py:40
  (1 shorter events, 0.0 us)
Async XLA Ops:
  6.5 43.5 %copy-start = (s32[128,2]{0,1:T(2,128)S(1)}, s32[128,2]{0,1:T(2,128)}, u32[]{:S(2)}) copy-start(s32[128,2]{0,1:T(2,128)} %param.9) | copy-start | bytes 3076
  6.5 44.7 %copy-start.3 = (s32[2,16]{1,0:T(2,128)S(1)}, s32[2,16]{1,0:T(2,128)}, u32[]{:S(2)}) copy-start(s32[2,16]{1,0:T(2,128)} %param.10) | copy-start | bytes 388
  6.5 52.3 %copy-start.1 = (bf16[1024,1024]{1,0:T(8,128)(2,1)S(1)}, bf16[1024,1024]{1,0:T(8,128)(2,1)}, u32[]{:S(2)}) copy-start(bf16[1024,1024]{1,0:T(8,128)(2,1)} %tile_ref.1) | copy-start | bytes 6291460
  6.5 52.3 %all-gather.3.cloned.1.call-start = ((), (), s32[]{:S(2)}) async-start(), calls=%async_computation.1 | async-start | bytes 2359296 | tf_op jit(solution)/shard_map/all_gather | solution.py:64
  48.1 4.7 %collective-permute-start = (bf16[512,1024]{1,0:T(8,128)(2,1)S(1)}, bf16[512,1024]{1,0:T(8,128)(2,1)}, u32[]{:S(2)}, u32[]{:S(2)}) collective-permute-start(bf16[512,1024]{1,0:T(8,128)(2,1)S(1)} %bitcast.5), channel_id=1, source_target_pairs={{0,8},{8,0},{16,24},{24,16},{32,40},{40,32},{48,56},{56,48},{64,72... | collective-permute-start | bytes 3145736 | tf_op jit(solution)/shard_map/ppermute | solution.py:76
  58.8 1.6 %copy-start.2 = (bf16[2,512,1024]{2,1,0:T(8,128)(2,1)S(1)}, bf16[2,512,1024]{2,1,0:T(8,128)(2,1)}, u32[]{:S(2)}) copy-start(bf16[2,512,1024]{2,1,0:T(8,128)(2,1)} %all-gather.3.cloned.1.call-done.p_ref) | copy-start | bytes 6291460
Sparse Core Ops, SparseCore 0:
  9.4 49.3 all-gather.2

commit v2 on v1

v2 whole, which is shorter than its diff:
```python
import functools

import jax
import jax.numpy as jnp
from jax import lax
from jax.experimental import pallas as pl
from jax.experimental.pallas import tpu as pltpu
from jax.sharding import PartitionSpec as P

B = 512
PANELS = 2
CORES = 2
P_SCALE = 2.0**17
H_SCALE = 2.0**12
SMALL = 2.0**-14
FAR = 2.0**29


def finish(flags, kept_ref, other_ref, tile_ref, out_ref):
    rows = out_ref.shape[0]
    start = pl.program_id(0) * rows
    row_block = start // B
    p_rows = pl.ds(pl.multiple_of(start, rows), rows)
    depth = kept_ref.shape[0] // PANELS

    def write(cols, p_ref, h_ref, inner):
        value = 2.0 * tile_ref[:, cols].astype(jnp.float32)
        if inner is not None:
            value -= lax.dot_general(
                p_ref[inner, p_rows],
                h_ref[inner, cols],
                (((0,), (0,)), ((), ())),
                preferred_element_type=jnp.float32,
            )
        for col in range(cols.start // B, cols.stop // B):
            keep = flags[9 + row_block * 2 + col].astype(jnp.float32)
            part = slice(col * B - cols.start, (col + 1) * B - cols.start)
            out_ref[:, col * B : (col + 1) * B] = (keep * value[:, part]).astype(out_ref.dtype)

    inners = [None, slice(0, depth), slice(depth, 2 * depth), slice(0, 2 * depth)]
    width = out_ref.shape[1]
    col_count = width // B
    states = []
    for col in range(col_count):
        alive = [flags[1 + row_block * 2 + p] * flags[5 + p * 2 + col] for p in range(PANELS)]
        states.append(alive[0] + 2 * alive[1])
    full = (states[0] == 3) & (states[1] == 3)
    for core, refs in enumerate([(kept_ref, other_ref), (other_ref, kept_ref)]):
        here = flags[0] == core
        pl.when(here & full)(functools.partial(write, slice(0, width), *refs, inners[3]))
        for col in range(col_count):
            cols = slice(col * B, (col + 1) * B)
            for case, inner in enumerate(inners):
                pl.when(here & jnp.logical_not(full) & (states[col] == case))(
                    functools.partial(write, cols, *refs, inner)
                )


def purify(flags, kept, other, p_tile):
    rows = 512
    height, width = p_tile.shape
    inner = kept.shape[0]
    whole = pl.BlockSpec(memory_space=pltpu.VMEM)
    return pl.pallas_call(
        finish,
        out_shape=jax.ShapeDtypeStruct((height, width), p_tile.dtype),
        grid=(height // rows,),
        in_specs=[
            pl.BlockSpec(memory_space=pltpu.SMEM),
            whole,
            whole,
            pl.BlockSpec((rows, width), lambda i: (i, 0)),
        ],
        out_specs=pl.BlockSpec((rows, width), lambda i: (i, 0)),
        compiler_params=pltpu.CompilerParams(vmem_limit_bytes=24 << 20),
        cost_estimate=pl.CostEstimate(
            flops=2 * inner * height * width,
            bytes_accessed=2 * (inner * (height + width) + 2 * height * width),
            transcendentals=0,
        ),
    )(flags, kept, other, p_tile)


def local(p_panel, h_panel, p_tile, p_mask, h_mask, keep_mask, *, row_devices, col_devices):
    row_index = lax.axis_index("row")
    col_index = lax.axis_index("col")
    core = row_index % CORES
    line = row_devices // col_devices
    swap = [(d, d ^ 1) for d in range(row_devices)]

    p_other = lax.ppermute(p_panel, "row", swap)
    lines = [[line * y + d for d in range(line)] for y in range(col_devices)]
    h_line = lax.all_gather(h_panel, "row", axis=1, axis_index_groups=lines, tiled=True)

    is_p = core == 0
    scale = jnp.where(is_p, P_SCALE, H_SCALE).astype(jnp.float32)
    unscale = jnp.where(is_p, 1 / P_SCALE, 1 / H_SCALE).astype(jnp.float32)
    far_unscale = jnp.where(is_p, 1 / (P_SCALE * FAR), 1 / (H_SCALE * FAR)).astype(jnp.float32)
    give = jnp.where(is_p, jnp.stack([p_panel, p_other]), jnp.stack([h_line, h_line]))
    near = give.astype(jnp.float32) * scale
    far = near * (FAR * (1 + 1 / 1024))
    far = jnp.where(jnp.abs(far) >= SMALL, far, 0.0)
    give = jnp.where(jnp.abs(near) >= SMALL, near, far).astype(jnp.float16)
    groups = [
        [row * col_devices + c for c in range(col_devices)] for row in range(0, row_devices, CORES)
    ] + [
        [(line * y + x) * col_devices + c for y in range(col_devices)]
        for x in range(1, line, CORES)
        for c in range(col_devices)
    ]
    got = lax.all_gather(give, ("row", "col"), axis=2, axis_index_groups=groups, tiled=True)

    def decode(part):
        value = part.astype(jnp.float32)
        top = lax.reduce_precision(value, 8, 7)
        return (top * jnp.where(value == top, unscale, far_unscale)).astype(p_tile.dtype)

    sent, got, p_mask, h_mask, keep_mask = lax.optimization_barrier(
        (decode(got[1]), got, p_mask, h_mask, keep_mask)
    )
    other = lax.ppermute(sent, "row", swap)
    kept = decode(lax.dynamic_index_in_dim(got, core, 0, keepdims=False))

    row_count = p_tile.shape[0] // B
    col_count = p_tile.shape[1] // B
    row_first = row_index * row_count
    col_first = col_index * col_count
    flags = jnp.concatenate(
        [
            core[None].astype(jnp.int32),
            lax.dynamic_slice_in_dim(p_mask, row_first, row_count, 0).reshape(-1),
            lax.dynamic_slice_in_dim(h_mask, col_first, col_count, 1).reshape(-1),
            lax.dynamic_slice(keep_mask, (row_first, col_first), (row_count, col_count)).reshape(-1),
        ]
    )
    flat = lambda a: a.reshape(-1, a.shape[-1])
    return purify(flags, flat(kept), flat(other), p_tile)


def solution(mesh):
    in_specs = (P(None, "col", "row"), P(None, "row", "col"), P("row", "col"), P(), P(), P())
    out_specs = P("row", "col")
    body = functools.partial(local, row_devices=mesh.shape["row"], col_devices=mesh.shape["col"])
    return jax.shard_map(body, mesh=mesh, in_specs=in_specs, out_specs=out_specs, check_vma=False)
```

time: 73.1 us -> 70.7 us (0.967)
  the two profiles are of different devices: /device:TPU:2 before, /device:TPU:1 now
where the time goes in v2:
time: 70.7 us; the launch traced here: 69.8 us
  blocking collectives  40 us (57%)
  starting transfers between devices  16.6 us (23%)
  local copies, waits for them, and re-layouts  5.59 us (8%)
  other arithmetic  4.52 us (6%)
  Pallas kernels  3 us (4%)
    all_gather x1, blocking collectives, local(): lax.all_gather(give, ('row', 'col'), axis=2, axis_index_groups=groups, ti...  27.1 us
    all_gather x1, blocking collectives, local(): lax.all_gather(h_panel, 'row', axis=1, axis_index_groups=lines, tiled=True)  12.9 us
    ppermute x1, starting transfers between devices, local(): p_other = lax.ppermute(p_panel, 'row', swap)  8.91 us
    ppermute x1, starting transfers between devices, local(): other = lax.ppermute(sent, 'row', swap)  7.71 us
    convert_element_type x2, other arithmetic, decode(): (top * jnp.where(value == top, unscale, far_unscale)).astype(p_tile.dtype)  3.03 us
    pallas_call x1, Pallas kernels, purify(): pl.pallas_call(finish, out_shape=jax.ShapeDtypeStruct((height, width), p_...  3 us
    dynamic_slice x1, local copies, waits for them, and re-layouts, local(): kept = decode(lax.dynamic_index_in_dim(got, core, 0, keepdims=False))  2.29 us
    unnamed x8, local copies, waits for them, and re-layouts  1.95 us
  transfers between devices with their start and end apart: 2, of which 0 were waited for; matrix products, arithmetic and copies ran while one was open for 7% of the time, Pallas kernels for 0%

profile of v2, /device:TPU:1, one launch (start us, length us, event | category | flops | bytes accessed | tf_op | source)
XLA Modules:
  0.0 69.8 jit_solution(9621153682630367689)
XLA Ops:
  0.0 0.0 copy-start
  0.0 8.9 %collective-permute-start = (bf16[2,64,1024]{2,1,0:T(8,128)(2,1)}, bf16[2,64,1024]{2,1,0:T(8,128)(2,1)S(1)}, u32[]{:S(2)}, u32[]{:S(2)}) collective-permute-start(bf16[2,64,1024]{2,1,0:T(8,128)(2,1)} %param.6), channel_id=1, source_target_pairs={{0,8},{8,0},{16,24},{24,16},{32,40},{40,32},{48,56},{56,48},{64,72... | collective-permute-start | bytes 786440 | tf_op jit(solution)/shard_map/ppermute | solution.py:91
  8.9 12.9 %all_gather.6 = bf16[2,64,1024]{2,1,0:T(8,128)(2,1)S(1)} all-gather(bf16[2,8,1024]{2,1,0:T(8,128)(2,1)} %param.7), channel_id=1, replica_groups={{0,8,16,24,32,40,48,56},{64,72,80,88,96,104,112,120},{128,136,144,152,1..., dimensions={1}, use_global_device_ids=true | all-gather | bytes 294912 | tf_op jit(solution)/shard_map/all_gather | solution.py:93
  21.8 0.0 collective-permute-done
  21.8 1.4 %select_convert_fusion = f16[2,2,64,1024]{3,2,1,0:T(8,128)(2,1)S(1)} fusion(bf16[1,2,64,1024]{3,2,1,0:T(8,128)(2,1)S(1)} %bitcast.16, bf16[1,2,64,1024]{3,2,1,0:T(8,128)(2,1)} %bitcast.15, bf16[1,2,64,1024]{3,2,1,0:T(8,128)(2,1)S(1)} %bitcast.14, f32[]{:T(128)S(6)} %select_n.56, pred[]{:T(512)S(6)} %eq.12), kind=kLoop, calls=%fused_computation.7 | loop fusion | flops 3407872 | bytes 1310725 | tf_op jit(solution)/shard_map/convert_element_type | solution.py:103
  23.3 0.0 copy-start.3
  23.3 27.1 %all-gather.1 = f16[2,2,512,1024]{3,2,1,0:T(8,128)(2,1)S(1)} all-gather(f16[2,2,64,1024]{3,2,1,0:T(8,128)(2,1)S(1)} %select_convert_fusion), channel_id=1, replica_groups={{0,1,2,3,4,5,6,7},{16,17,18,19,20,21,22,23},{32,33,34,35,36,37,38,39},{..., dimensions={2}, use_global_device_ids=true | all-gather | bytes 4718592 | tf_op jit(solution)/shard_map/all_gather | solution.py:111
  50.4 0.0 copy-start.2
  50.4 1.9 %copy-done.2 = f16[2,2,512,1024]{3,2,1,0:T(8,128)(2,1)} copy-done((f16[2,2,512,1024]{3,2,1,0:T(8,128)(2,1)}, f16[2,2,512,1024]{3,2,1,0:T(8,128)(2,1)S(1)}, u32[]{:S(2)}) %copy-start.2) | copy-done | bytes 4194328
  52.3 2.1 %fusion = bf16[2,512,1024]{2,1,0:T(8,128)(2,1)} fusion(f16[2,2,512,1024]{3,2,1,0:T(8,128)(2,1)S(1)} %all-gather.1, f32[]{:T(128)S(6)} %select_n.60, f32[]{:T(128)S(6)} %select_n.59), kind=kLoop, calls=%fused_computation.4 | loop fusion | flops 6291456 | bytes 4194312 | tf_op jit(solution)/shard_map/convert_element_type | solution.py:116
  54.4 7.7 %collective-permute-start.1 = (bf16[2,512,1024]{2,1,0:T(8,128)(2,1)}, bf16[2,512,1024]{2,1,0:T(8,128)(2,1)S(1)}, u32[]{:S(2)}, u32[]{:S(2)}) collective-permute-start(bf16[2,512,1024]{2,1,0:T(8,128)(2,1)} %fusion), channel_id=1, source_target_pairs={{0,8},{8,0},{16,24},{24,16},{32,40},{40,32},{48,56},{56,48},{64,72... | collective-permute-start | bytes 6291464 | tf_op jit(solution)/shard_map/ppermute | solution.py:121
  62.1 0.0 copy-done
  62.1 0.1 constant_dynamic-slice_fusion.2
  62.2 0.1 copy.7
  62.3 0.1 reshape.18
  62.4 0.8 %dynamic_slice.15 = s32[2,2]{0,1:T(2,128)S(1)} dynamic-slice(s32[128,16]{0,1:T(8,128)} %param.11, s32[]{:T(128)S(6)} %select_n.62, s32[]{:T(128)S(6)} %select_n.63), dynamic_slice_sizes={2,2} | dynamic-slice | bytes 36 | tf_op jit(solution)/shard_map/dynamic_slice | solution.py:133
  63.2 0.1 copy.8
  63.3 0.1 reshape.20
  63.3 0.0 copy-done.3
  63.3 0.1 constant_dynamic-slice_fusion.1
  63.4 0.1 reshape.19
  63.5 0.1 pad_add_fusion.flags
  63.6 0.0 copy-start.1
  63.6 2.3 %constant_dynamic-slice_fusion = f16[1,2,512,1024]{3,2,1,0:T(8,128)(2,1)S(1)} fusion(f16[2,2,512,1024]{3,2,1,0:T(8,128)(2,1)} %copy-done.2, s32[]{:T(128)S(6)} %select_n.64), kind=kLoop, calls=%fused_computation.11 | loop fusion | bytes 4194308 | tf_op jit(solution)/shard_map/jit(dynamic_index_in_dim)/dynamic_slice | solution.py:122
  65.9 0.9 %fusion.1.kept_ref = bf16[1024,1024]{1,0:T(8,128)(2,1)S(1)} fusion(f16[1,2,512,1024]{3,2,1,0:T(8,128)(2,1)S(1)} %constant_dynamic-slice_fusion, f32[]{:T(128)S(6)} %select_n.60, f32[]{:T(128)S(6)} %select_n.59), kind=kLoop, calls=%fused_computation.5 | loop fusion | flops 6291456 | bytes 4194312 | tf_op jit(solution)/shard_map/convert_element_type | solution.py:116
  66.8 0.0 collective-permute-done.1
  66.8 0.0 copy-done.1
  66.8 3.0 %shard_map.64 = bf16[1024,1024]{1,0:T(8,128)(2,1)} custom-call(s32[13]{0:T(128)S(1)} %pad_add_fusion.flags, bf16[1024,1024]{1,0:T(8,128)(2,1)S(1)} %fusion.1.kept_ref, bf16[1024,1024]{1,0:T(8,128)(2,1)S(1)} %bitcast.13, bf16[1024,1024]{1,0:T(8,128)(2,1)S(1)} %copy-done.1), custom_call_target="tpu_custom_call" | custom-call | flops 2147483648 | bytes 8388608 | tf_op jit(solution)/shard_map/pallas_call | solution.py:64
Async XLA Ops:
  0.0 62.1 %copy-start = (s32[128,2]{0,1:T(2,128)S(1)}, s32[128,2]{0,1:T(2,128)}, u32[]{:S(2)}) copy-start(s32[128,2]{0,1:T(2,128)} %param.9) | copy-start | bytes 3076
  0.0 21.8 %collective-permute-start = (bf16[2,64,1024]{2,1,0:T(8,128)(2,1)}, bf16[2,64,1024]{2,1,0:T(8,128)(2,1)S(1)}, u32[]{:S(2)}, u32[]{:S(2)}) collective-permute-start(bf16[2,64,1024]{2,1,0:T(8,128)(2,1)} %param.6), channel_id=1, source_target_pairs={{0,8},{8,0},{16,24},{24,16},{32,40},{40,32},{48,56},{56,48},{64,72... | collective-permute-start | bytes 786440 | tf_op jit(solution)/shard_map/ppermute | solution.py:91
  23.3 40.1 %copy-start.3 = (s32[2,16]{1,0:T(2,128)S(1)}, s32[2,16]{1,0:T(2,128)}, u32[]{:S(2)}) copy-start(s32[2,16]{1,0:T(2,128)} %param.10) | copy-start | bytes 388
  50.4 1.9 %copy-start.2 = (f16[2,2,512,1024]{3,2,1,0:T(8,128)(2,1)}, f16[2,2,512,1024]{3,2,1,0:T(8,128)(2,1)S(1)}, u32[]{:S(2)}) copy-start(f16[2,2,512,1024]{3,2,1,0:T(8,128)(2,1)S(1)} %all-gather.1) | copy-start | bytes 12582916
  54.4 12.4 %collective-permute-start.1 = (bf16[2,512,1024]{2,1,0:T(8,128)(2,1)}, bf16[2,512,1024]{2,1,0:T(8,128)(2,1)S(1)}, u32[]{:S(2)}, u32[]{:S(2)}) collective-permute-start(bf16[2,512,1024]{2,1,0:T(8,128)(2,1)} %fusion), channel_id=1, source_target_pairs={{0,8},{8,0},{16,24},{24,16},{32,40},{40,32},{48,56},{56,48},{64,72... | collective-permute-start | bytes 6291464 | tf_op jit(solution)/shard_map/ppermute | solution.py:121
  63.6 3.2 %copy-start.1 = (bf16[1024,1024]{1,0:T(8,128)(2,1)S(1)}, bf16[1024,1024]{1,0:T(8,128)(2,1)}, u32[]{:S(2)}) copy-start(bf16[1024,1024]{1,0:T(8,128)(2,1)} %tile_ref.1) | copy-start | bytes 6291460

commit v3 on v2

--- a/solution.py
+++ b/solution.py
@@ -72,7 +72,7 @@
             pl.BlockSpec((rows, width), lambda i: (i, 0)),
         ],
         out_specs=pl.BlockSpec((rows, width), lambda i: (i, 0)),
-        compiler_params=pltpu.CompilerParams(vmem_limit_bytes=24 << 20),
+        compiler_params=pltpu.CompilerParams(vmem_limit_bytes=50 << 20),
         cost_estimate=pl.CostEstimate(
             flops=2 * inner * height * width,
             bytes_accessed=2 * (inner * (height + width) + 2 * height * width),
@@ -110,16 +110,17 @@
     ]
     got = lax.all_gather(give, ("row", "col"), axis=2, axis_index_groups=groups, tiled=True)
 
-    def decode(part):
+    def decode(part, unscale, far_unscale):
         value = part.astype(jnp.float32)
         top = lax.reduce_precision(value, 8, 7)
         return (top * jnp.where(value == top, unscale, far_unscale)).astype(p_tile.dtype)
 
-    sent, got, p_mask, h_mask, keep_mask = lax.optimization_barrier(
-        (decode(got[1]), got, p_mask, h_mask, keep_mask)
+    sent, unscale, far_unscale, p_mask, h_mask, keep_mask = lax.optimization_barrier(
+        (decode(got[1], unscale, far_unscale), unscale, far_unscale, p_mask, h_mask, keep_mask)
     )
     other = lax.ppermute(sent, "row", swap)
-    kept = decode(lax.dynamic_index_in_dim(got, core, 0, keepdims=False))
+    kept = lax.dynamic_index_in_dim(got, core, 0, keepdims=False)
+    kept = decode(kept, unscale, far_unscale)
 
     row_count = p_tile.shape[0] // B
     col_count = p_tile.shape[1] // B

time: 70.7 us -> 70.6 us (level)
  Pallas kernels: 3 us -> 4.73 us
  other arithmetic: 4.52 us -> 3.2 us
    pallas_call x1, Pallas kernels: 3 us -> 4.73 us  [purify(): pl.pallas_call(finish, out_shape=jax.ShapeDtypeStruct((height, width), p_...]
    convert_element_type x2, other arithmetic: 3.03 us -> 1.7 us  [decode(): (top * jnp.where(value == top, unscale, far_unscale)).astype(p_tile.dtype)]
    unnamed x8 -> x6, local copies, waits for them, and re-layouts: 1.95 us -> 1.95 us
  transfers between devices with their start and end apart: 2 -> 2, of which waited for: 0 -> 0; matrix products, arithmetic and copies ran while one was open for 7% -> 6% of each run, Pallas kernels for 0% -> 0%
where the time goes in v3:
time: 70.6 us; the launch traced here: 70.1 us
  blocking collectives  40 us (57%)
  starting transfers between devices  16.6 us (24%)
  local copies, waits for them, and re-layouts  5.44 us (8%)
  Pallas kernels  4.73 us (7%)
  other arithmetic  3.2 us (5%)
    all_gather x1, blocking collectives, local(): lax.all_gather(give, ('row', 'col'), axis=2, axis_index_groups=groups, ti...  27.1 us
    all_gather x1, blocking collectives, local(): lax.all_gather(h_panel, 'row', axis=1, axis_index_groups=lines, tiled=True)  12.9 us
    ppermute x1, starting transfers between devices, local(): p_other = lax.ppermute(p_panel, 'row', swap)  8.91 us
    ppermute x1, starting transfers between devices, local(): other = lax.ppermute(sent, 'row', swap)  7.72 us
    pallas_call x1, Pallas kernels, purify(): pl.pallas_call(finish, out_shape=jax.ShapeDtypeStruct((height, width), p_...  4.73 us
    dynamic_slice x1, local copies, waits for them, and re-layouts, local(): kept = lax.dynamic_index_in_dim(got, core, 0, keepdims=False)  2.14 us
    unnamed x6, local copies, waits for them, and re-layouts  1.95 us
    convert_element_type x2, other arithmetic, decode(): (top * jnp.where(value == top, unscale, far_unscale)).astype(p_tile.dtype)  1.7 us
  transfers between devices with their start and end apart: 2, of which 0 were waited for; matrix products, arithmetic and copies ran while one was open for 6% of the time, Pallas kernels for 0%

profile of v3, /device:TPU:1, one launch (start us, length us, event | category | flops | bytes accessed | tf_op | source)
XLA Modules:
  0.0 70.1 jit_solution(15945858394547449656)
XLA Ops:
  0.0 0.0 copy-start
  0.0 8.9 %collective-permute-start = (bf16[2,64,1024]{2,1,0:T(8,128)(2,1)}, bf16[2,64,1024]{2,1,0:T(8,128)(2,1)S(1)}, u32[]{:S(2)}, u32[]{:S(2)}) collective-permute-start(bf16[2,64,1024]{2,1,0:T(8,128)(2,1)} %param.6), channel_id=1, source_target_pairs={{0,8},{8,0},{16,24},{24,16},{32,40},{40,32},{48,56},{56,48},{64,72... | collective-permute-start | bytes 786440 | tf_op jit(solution)/shard_map/ppermute | solution.py:91
  8.9 12.9 %all_gather.6 = bf16[2,64,1024]{2,1,0:T(8,128)(2,1)S(1)} all-gather(bf16[2,8,1024]{2,1,0:T(8,128)(2,1)} %param.7), channel_id=1, replica_groups={{0,8,16,24,32,40,48,56},{64,72,80,88,96,104,112,120},{128,136,144,152,1..., dimensions={1}, use_global_device_ids=true | all-gather | bytes 294912 | tf_op jit(solution)/shard_map/all_gather | solution.py:93
  21.8 0.0 collective-permute-done
  21.8 1.4 %select_convert_fusion = f16[2,2,64,1024]{3,2,1,0:T(8,128)(2,1)S(1)} fusion(bf16[1,2,64,1024]{3,2,1,0:T(8,128)(2,1)S(1)} %bitcast.15, bf16[1,2,64,1024]{3,2,1,0:T(8,128)(2,1)} %bitcast.14, bf16[1,2,64,1024]{3,2,1,0:T(8,128)(2,1)S(1)} %bitcast.13, f32[]{:T(128)S(6)} %select_n.56, pred[]{:T(512)S(6)} %eq.12), kind=kLoop, calls=%fused_computation.7 | loop fusion | flops 3407872 | bytes 1310725 | tf_op jit(solution)/shard_map/convert_element_type | solution.py:103
  23.3 0.0 copy-start.2
  23.3 27.1 %all-gather.1 = f16[2,2,512,1024]{3,2,1,0:T(8,128)(2,1)S(1)} all-gather(f16[2,2,64,1024]{3,2,1,0:T(8,128)(2,1)S(1)} %select_convert_fusion), channel_id=1, replica_groups={{0,1,2,3,4,5,6,7},{16,17,18,19,20,21,22,23},{32,33,34,35,36,37,38,39},{..., dimensions={2}, use_global_device_ids=true | all-gather | bytes 4718592 | tf_op jit(solution)/shard_map/all_gather | solution.py:111
  50.4 0.0 copy-start.1
  50.4 1.9 %copy-done.1 = f16[2,2,512,1024]{3,2,1,0:T(8,128)(2,1)} copy-done((f16[2,2,512,1024]{3,2,1,0:T(8,128)(2,1)}, f16[2,2,512,1024]{3,2,1,0:T(8,128)(2,1)S(1)}, u32[]{:S(2)}) %copy-start.1) | copy-done | bytes 4194328
  52.3 0.8 %fusion = bf16[2,512,1024]{2,1,0:T(8,128)(2,1)S(1)} fusion(f16[2,2,512,1024]{3,2,1,0:T(8,128)(2,1)S(1)} %all-gather.1, f32[]{:T(128)S(6)} %select_n.60, f32[]{:T(128)S(6)} %select_n.59), kind=kLoop, calls=%fused_computation.4 | loop fusion | flops 6291456 | bytes 4194312 | tf_op jit(solution)/shard_map/convert_element_type | solution.py:116
  53.1 7.7 %collective-permute-start.1 = (bf16[2,512,1024]{2,1,0:T(8,128)(2,1)S(1)}, bf16[2,512,1024]{2,1,0:T(8,128)(2,1)}, u32[]{:S(2)}, u32[]{:S(2)}) collective-permute-start(bf16[2,512,1024]{2,1,0:T(8,128)(2,1)S(1)} %fusion), channel_id=1, source_target_pairs={{0,8},{8,0},{16,24},{24,16},{32,40},{40,32},{48,56},{56,48},{64,72... | collective-permute-start | bytes 6291464 | tf_op jit(solution)/shard_map/ppermute | solution.py:121
  60.8 0.8 %dynamic_slice.15 = s32[2,2]{0,1:T(2,128)S(1)} dynamic-slice(s32[128,16]{0,1:T(8,128)} %param.11, s32[]{:T(128)S(6)} %select_n.62, s32[]{:T(128)S(6)} %select_n.63), dynamic_slice_sizes={2,2} | dynamic-slice | bytes 36 | tf_op jit(solution)/shard_map/dynamic_slice | solution.py:134
  61.6 0.1 copy.8
  61.7 0.1 reshape.20
  61.8 0.0 copy-done
  61.8 0.1 constant_dynamic-slice_fusion.1
  61.9 0.1 reshape.19
  61.9 0.0 copy-done.2
  61.9 0.1 constant_dynamic-slice_fusion.2
  62.0 0.1 copy.7
  62.1 0.1 reshape.18
  62.2 0.1 pad_add_fusion.flags
  62.3 2.1 %constant_dynamic-slice_fusion = f16[1,2,512,1024]{3,2,1,0:T(8,128)(2,1)S(1)} fusion(f16[2,2,512,1024]{3,2,1,0:T(8,128)(2,1)} %copy-done.1, s32[]{:T(128)S(6)} %select_n.64), kind=kLoop, calls=%fused_computation.11 | loop fusion | bytes 4194308 | tf_op jit(solution)/shard_map/jit(dynamic_index_in_dim)/dynamic_slice | solution.py:122
  64.4 0.9 %fusion.1.kept_ref = bf16[1024,1024]{1,0:T(8,128)(2,1)S(1)} fusion(f16[1,2,512,1024]{3,2,1,0:T(8,128)(2,1)S(1)} %constant_dynamic-slice_fusion, f32[]{:T(128)S(6)} %select_n.60, f32[]{:T(128)S(6)} %select_n.59), kind=kLoop, calls=%fused_computation.5 | loop fusion | flops 6291456 | bytes 4194312 | tf_op jit(solution)/shard_map/convert_element_type | solution.py:116
  65.3 0.0 collective-permute-done.1
  65.4 4.7 %shard_map.64 = bf16[1024,1024]{1,0:T(8,128)(2,1)} custom-call(s32[13]{0:T(128)S(1)} %pad_add_fusion.flags, bf16[1024,1024]{1,0:T(8,128)(2,1)S(1)} %fusion.1.kept_ref, bf16[1024,1024]{1,0:T(8,128)(2,1)} %bitcast.8.other_ref, bf16[1024,1024]{1,0:T(8,128)(2,1)} %tile_ref.1), custom_call_target="tpu_custom_call" | custom-call | flops 2147483648 | bytes 8388608 | tf_op jit(solution)/shard_map/pallas_call | solution.py:64
Async XLA Ops:
  0.0 61.8 %copy-start = (s32[2,16]{1,0:T(2,128)S(1)}, s32[2,16]{1,0:T(2,128)}, u32[]{:S(2)}) copy-start(s32[2,16]{1,0:T(2,128)} %param.10) | copy-start | bytes 388
  0.0 21.8 %collective-permute-start = (bf16[2,64,1024]{2,1,0:T(8,128)(2,1)}, bf16[2,64,1024]{2,1,0:T(8,128)(2,1)S(1)}, u32[]{:S(2)}, u32[]{:S(2)}) collective-permute-start(bf16[2,64,1024]{2,1,0:T(8,128)(2,1)} %param.6), channel_id=1, source_target_pairs={{0,8},{8,0},{16,24},{24,16},{32,40},{40,32},{48,56},{56,48},{64,72... | collective-permute-start | bytes 786440 | tf_op jit(solution)/shard_map/ppermute | solution.py:91
  23.3 38.7 %copy-start.2 = (s32[128,2]{0,1:T(2,128)S(1)}, s32[128,2]{0,1:T(2,128)}, u32[]{:S(2)}) copy-start(s32[128,2]{0,1:T(2,128)} %param.9) | copy-start | bytes 3076
  50.4 1.9 %copy-start.1 = (f16[2,2,512,1024]{3,2,1,0:T(8,128)(2,1)}, f16[2,2,512,1024]{3,2,1,0:T(8,128)(2,1)S(1)}, u32[]{:S(2)}) copy-start(f16[2,2,512,1024]{3,2,1,0:T(8,128)(2,1)S(1)} %all-gather.1) | copy-start | bytes 12582916
  53.1 12.3 %collective-permute-start.1 = (bf16[2,512,1024]{2,1,0:T(8,128)(2,1)S(1)}, bf16[2,512,1024]{2,1,0:T(8,128)(2,1)}, u32[]{:S(2)}, u32[]{:S(2)}) collective-permute-start(bf16[2,512,1024]{2,1,0:T(8,128)(2,1)S(1)} %fusion), channel_id=1, source_target_pairs={{0,8},{8,0},{16,24},{24,16},{32,40},{40,32},{48,56},{56,48},{64,72... | collective-permute-start | bytes 6291464 | tf_op jit(solution)/shard_map/ppermute | solution.py:121
